TPU v7x, 32 devices: a whole 2x2x4 slice. The times are simulated.
32 devices in a mesh: section: 4 (over y, core), kv: 4 (over z), tp: 2 (over x).
Axes of the slice: x: 2, y: 2, z: 4, core: 2. Of those that a mesh axis runs over, the one named last changes fastest.
Arguments:
- patches: bfloat16 [32768, 1152], P(('section', 'kv'), 'tp'), may hold values from -6 to 6
- vis_gain: float32 [1152], replicated, may hold values from 0.1 to 1.9
- vis_bias: float32 [1152], replicated, may hold values from -3 to 3
- w_proj: bfloat16 [1152, 4608], P('section', 'tp')
- b_proj: float32 [4608], P('tp'), may hold values from -12 to 12
- rms_gain: float32 [4608], P('tp'), may hold values from 0.1 to 1.9
- w_kv: bfloat16 [4608, 2, 1024], P('tp'), may hold values from -0.09375 to 0.09375
- queries: bfloat16 [16, 2048], P('section', 'tp'), may hold values from -18 to 18
- cache: bfloat16 [256, 128, 2, 1024], P(('section', 'kv'), None, None, 'tp'), may hold values from -6 to 6
- cache_lengths: int32 [4, 4], P('section'), may hold values from 1 to 7296, 7680 in all within a row
- slot_page: int32 [4, 64], P('section', 'kv'), may hold values from 0 to 63, each once within a row
- page_owner: int32 [4, 64], replicated, may hold values from 0 to 3, as said below
- image_request: int32 [4, 2], P('section'), may hold values from 0 to 3
Outputs:
- new_pages: bfloat16 [512, 128, 2, 1024], P(('section', 'kv'), None, None, 'tp')
- attended: bfloat16 [16, 2048], P('section', 'tp')
Inputs may be any that keep to these rules, and one draw needn't show every extreme that they name: `page_owner`: from each source's 16 pages at most 8 go to any one owner; in every group one owner receives exactly 8 pages from every source.
All inputs are finite; a program needn't handle non-finite values.
Results may differ from a plain program's by a relative error of at most 0.0063.
Values may be sent and summed in bfloat16 or wider, within the bound.
A program may use at most 128 MiB of HBM per device.

v0:
```python
import jax
import jax.numpy as jnp
from jax import lax
from jax.sharding import PartitionSpec as P

HEAD_DIM = 128
IMAGE_PAGES = 32


query_scale = 1.0 / 12.0
softcap = 50.0
epsilon = 1e-06


def from_behind(value, axis, steps):
    count = lax.axis_size(axis)
    pairs = [(source, (source + steps) % count) for source in range(count)]
    return lax.ppermute(value, axis, pairs)


def block_ranks(owners):
    per_block = owners.shape[1]
    same_owner = owners[:, :, None] == owners[:, None, :]
    earlier = jnp.arange(per_block)[None, :] < jnp.arange(per_block)[:, None]
    return jnp.sum((same_owner & earlier[None, :, :]).astype(jnp.int32), axis=2)


def attend_part(query_grid, page_store, token_mask):
    slot_count = page_store.shape[0]
    page_len = page_store.shape[1]
    head_count = page_store.shape[3] // HEAD_DIM
    keys = page_store[:, :, 0, :].reshape(slot_count * page_len, head_count, HEAD_DIM)
    values = page_store[:, :, 1, :].reshape(slot_count * page_len, head_count, HEAD_DIM)
    raw_scores = jnp.einsum("rkgd,tkd->rkgt", query_grid, keys, preferred_element_type=jnp.float32)
    capped = softcap * jnp.tanh(raw_scores * query_scale / softcap)
    allowed = token_mask.reshape(slot_count * page_len, -1).T
    weights = jnp.where(allowed[:, None, None, :], jnp.exp(capped), jnp.float32(0.0))
    totals = jnp.sum(weights, axis=3)
    weighted = jnp.einsum(
        "rkgt,tkd->rkgd", weights.astype(jnp.bfloat16), values, preferred_element_type=jnp.float32
    )
    return (totals, weighted)


def per_device(
    patches,
    vis_gain,
    vis_bias,
    w_proj,
    b_proj,
    rms_gain,
    w_kv,
    queries,
    cache,
    cache_lengths,
    slot_page,
    page_owner,
    image_request,
):
    kv_count = lax.axis_size("kv")
    section_count = lax.axis_size("section")
    section_idx = lax.axis_index("section")
    kv_idx = lax.axis_index("kv")
    row_count = patches.shape[0]
    page_len = cache.shape[1]
    pages_dev = row_count // page_len
    capacity = max(2, (2 * pages_dev + kv_count - 1) // kv_count)
    recv_slots = kv_count * capacity
    gathered = lax.all_gather(patches, "tp", axis=1, tiled=True).astype(jnp.float32)
    row_mean = jnp.mean(gathered, axis=1, keepdims=True)
    centred = gathered - row_mean
    variance = jnp.mean(centred * centred, axis=1, keepdims=True)
    x_norm = (centred * lax.rsqrt(variance + epsilon) * vis_gain + vis_bias).astype(jnp.bfloat16)
    projected = (
        jnp.dot(
            x_norm,
            lax.all_gather(w_proj, "section", axis=0, tiled=True),
            preferred_element_type=jnp.float32,
        )
        + b_proj
    )
    squares = lax.psum(jnp.sum(projected * projected, axis=1), "tp")
    full_width = projected.shape[1] * lax.axis_size("tp")
    hidden = (projected * lax.rsqrt(squares / full_width + epsilon)[:, None] * rms_gain).astype(
        jnp.bfloat16
    )
    partial_kv = jnp.einsum("nd,dcf->ncf", hidden, w_kv, preferred_element_type=jnp.float32)
    image_kv = lax.psum_scatter(partial_kv, "tp", scatter_dimension=2, tiled=True)
    kv_pages = image_kv.astype(jnp.bfloat16).reshape(pages_dev, page_len, 2, image_kv.shape[2])
    next_group = (section_idx + 1) % section_count
    owners = lax.dynamic_index_in_dim(page_owner, next_group, 0, keepdims=False).reshape(
        kv_count, pages_dev
    )
    page_ranks = block_ranks(owners)
    my_owner = lax.dynamic_index_in_dim(owners, kv_idx, 0, keepdims=False)
    my_rank = lax.dynamic_index_in_dim(page_ranks, kv_idx, 0, keepdims=False)
    target = my_owner * capacity + my_rank
    placing = (jnp.arange(recv_slots)[:, None] == target[None, :]).astype(jnp.bfloat16)
    exchanged = lax.all_to_all(
        jnp.einsum("jp,ptcf->jtcf", placing, kv_pages, preferred_element_type=jnp.float32).astype(
            jnp.bfloat16
        ),
        "kv",
        split_axis=0,
        concat_axis=0,
        tiled=True,
    )
    new_pages = from_behind(exchanged, "section", 1)
    req_count = queries.shape[0]
    kv_heads_dev = cache.shape[3] // HEAD_DIM
    group_size = queries.shape[1] // HEAD_DIM // kv_heads_dev
    query_grid = queries.reshape(req_count, kv_heads_dev, group_size, HEAD_DIM)
    lengths = cache_lengths[0]
    page_counts = (lengths + page_len - 1) // page_len
    starts = jnp.cumsum(page_counts) - page_counts
    slot_ids = slot_page[0]
    within = slot_ids[:, None] - starts[None, :]
    inside = (within >= 0) & (within < page_counts[None, :])
    valid = jnp.where(inside, jnp.clip(lengths[None, :] - within * page_len, 0, page_len), 0)
    cache_mask = jnp.arange(page_len)[None, :, None] < valid[:, None, :]
    cache_totals, cache_weighted = attend_part(query_grid, cache, cache_mask)
    own_owners = lax.dynamic_index_in_dim(page_owner, section_idx, 0, keepdims=False).reshape(
        kv_count, pages_dev
    )
    own_ranks = block_ranks(own_owners)
    slot_of = (jnp.arange(kv_count)[:, None] * capacity + own_ranks).reshape(-1)
    arrives_here = own_owners.reshape(-1) == kv_idx
    image_count = image_request.shape[1]
    image_of = jnp.arange(kv_count * pages_dev) // IMAGE_PAGES
    request_row = image_request[0]
    page_request = jnp.sum(
        jnp.where(image_of[:, None] == jnp.arange(image_count)[None, :], request_row[None, :], 0),
        axis=1,
    )
    matched = arrives_here[None, :] & (slot_of[None, :] == jnp.arange(recv_slots)[:, None])
    request_hit = page_request[:, None] == jnp.arange(req_count)[None, :]
    slot_request = jnp.any(matched[:, :, None] & request_hit[None, :, :], axis=1)
    image_mask = jnp.broadcast_to(slot_request[:, None, :], (recv_slots, page_len, req_count))
    image_totals, image_weighted = attend_part(query_grid, new_pages, image_mask)
    totals, weighted = lax.psum(
        (cache_totals + image_totals, cache_weighted + image_weighted), "kv"
    )
    attended = (weighted / totals[..., None]).astype(jnp.bfloat16).reshape(req_count, -1)
    return (new_pages, attended)


def solution(mesh):
    in_specs = (
        P(("section", "kv"), "tp"),
        P(),
        P(),
        P("section", "tp"),
        P("tp"),
        P("tp"),
        P("tp", None, None),
        P("section", "tp"),
        P(("section", "kv"), None, None, "tp"),
        P("section", None),
        P("section", "kv"),
        P(),
        P("section", None),
    )
    out_specs = (P(("section", "kv"), None, None, "tp"), P("section", "tp"))
    return jax.shard_map(
        per_device, mesh=mesh, in_specs=in_specs, out_specs=out_specs, check_vma=False
    )
```

profile of v0, /device:TPU:25, one launch (start us, length us, event | category | flops | bytes accessed | tf_op | source)
XLA Modules:
  0.0 753.8 jit_solution(3433051893886293753)
XLA Ops:
  8.7 64.5 %all-gather.3.cloned.1.call-done = bf16[2048,1152]{0,1:T(8,128)(2,1)} async-done(((bf16[2048,576]{0,1:T(8,128)(2,1)}), bf16[2048,1152]{0,1:T(8,128)(2,1)}) %all-gather.3.cloned.1.call-update) | async-done | bytes 4718608 | tf_op jit(solution)/shard_map/all_gather | solution.py:69
  73.2 3.2 convert_reduce_fusion
  77.0 1.3 fusion.2
  78.3 37.8 %all-gather.5.cloned.1.call-done = bf16[1152,2304]{1,0:T(8,128)(2,1)} async-done(((bf16[288,2304]{1,0:T(8,128)(2,1)}), bf16[1152,2304]{1,0:T(8,128)(2,1)}) %all-gather.5.cloned.1.call-update) | async-done | bytes 5308432 | tf_op jit(solution)/shard_map/all_gather | solution.py:77
  116.0 20.8 %multiply_reduce_fusion = (f32[2048]{0:T(1024)S(1)}, f32[2048,2304]{1,0:T(8,128)}) fusion(f32[2304]{0:T(1024)S(1)} %copy-done.7, bf16[1152,2304]{1,0:T(8,128)(2,1)} %all-gather.5.cloned.1.call-done, bf16[2048,1152]{0,1:T(8,128)(2,1)} %all-gather.3.cloned.1.call-done, f32[1152]{0:T(1024)S(1)} %copy-done.9, f32[1152]{0:T(1024)S(1)} %copy-done.10, ...), kind=kOutput, calls=%fused_computation.1 | convolution fusion | flops 10899945472 | bytes 28944384 | tf_op jit(solution)/shard_map/dot_general | solution.py:75
  136.9 3.8 psum.21
  140.7 29.6 %fusion.7 = f32[2048,2,1024]{2,0,1:T(8,128)} fusion(f32[2048,2304]{1,0:T(8,128)} %get-tuple-element.17, bf16[2304,2,1024]{2,1,0:T(2,128)(2,1)} %param.19, f32[2304]{0:T(1024)S(1)} %copy-done.8, f32[2048]{0:T(1024)S(1)} %add_rsqrt_fusion, f32[2304]{0:T(1024)S(1)} %copy-done.7), kind=kOutput, calls=%fused_computation.11 | convolution fusion | flops 19346227200 | bytes 45115392 | tf_op jit(solution)/shard_map/nd,dcf->ncf/dot_general | solution.py:87
  171.5 188.9 %reduce-scatter.2.cloned.1.call-done = f32[2048,2,512]{2,0,1:T(8,128)} async-done(((f32[2048,2,1024]{2,0,1:T(8,128)}), f32[2048,2,512]{2,0,1:T(8,128)}) %reduce-scatter.2.cloned.1.call-update) | async-done | bytes 8388624 | tf_op jit(solution)/shard_map/reduce_scatter | solution.py:88
  360.3 3.9 convert_element_type.35
  364.3 3.0 convolution_convert_fusion
  367.2 19.4 %copy.48 = bf16[32,128,2,512]{3,2,1,0:T(2,128)(2,1)S(1)} copy(bf16[32,128,2,512]{3,0,2,1:T(8,128)(2,1)S(1)} %convolution_convert_fusion) | data formatting | bytes 16777216 | tf_op jit(solution)/shard_map/convert_element_type | solution.py:100
  386.6 186.0 %all_to_all.5 = bf16[32,128,2,512]{3,2,1,0:T(2,128)(2,1)} all-to-all(bf16[32,128,2,512]{3,2,1,0:T(2,128)(2,1)S(1)} %copy.48), channel_id=1, replica_groups=mesh['section'=4,'kv'=4,'tp'=2] {'kv'}, dimensions={0} | all-to-all | bytes 16777216 | tf_op jit(solution)/shard_map/all_to_all | solution.py:99
  572.6 2.2 collective-permute-start
  574.9 20.3 %slice_reduce_fusion.3 = (bf16[16,128,512]{2,1,0:T(8,128)(2,1)}, bf16[16,128,512]{2,1,0:T(8,128)(2,1)}) fusion(bf16[16,128,2,512]{3,2,1,0:T(2,128)(2,1)S(1)} %copy-done.2), kind=kLoop, calls=%fused_computation.35 | loop fusion | bytes 8388608 | tf_op jit(solution)/shard_map/slice | solution.py:32
  595.1 2.6 reshape.238
  597.7 4.0 reshape.237
  602.7 2.3 fusion.62
  605.5 60.0 %collective-permute-done = bf16[32,128,2,512]{3,2,1,0:T(2,128)(2,1)} collective-permute-done((bf16[32,128,2,512]{3,2,1,0:T(2,128)(2,1)}, bf16[32,128,2,512]{3,2,1,0:T(2,128)(2,1)}, u32[]{:S(2)}, u32[]{:S(2)}) %collective-permute-start) | collective-permute-done | bytes 8388640 | tf_op jit(solution)/shard_map/ppermute | solution.py:18
  665.6 42.9 %slice_reduce_fusion = (bf16[32,128,512]{2,1,0:T(8,128)(2,1)}, bf16[32,128,512]{2,1,0:T(8,128)(2,1)}) fusion(bf16[32,128,2,512]{3,2,1,0:T(2,128)(2,1)} %collective-permute-done), kind=kLoop, calls=%fused_computation.16 | loop fusion | bytes 16777216 | tf_op jit(solution)/shard_map/slice | solution.py:32
  708.5 6.9 reshape.239
  715.4 6.9 reshape.240
  722.3 3.6 fusion.63
  726.7 12.0 %all-reduce = (f32[4,4,2,128]{3,0,2,1:T(4,128)S(1)}, f32[4,4,2]{0,2,1:T(2,128)S(1)}) all-reduce(f32[4,4,2,128]{3,0,2,1:T(4,128)S(1)} %fusion.42, f32[4,4,2]{0,2,1:T(2,128)S(1)} %add.127), channel_id=1, replica_groups=mesh['section'=4,'kv'=4,'tp'=2] {'kv'}, use_global_device_ids=true, to_apply=%region_10.11 | all-reduce | flops 4128 | bytes 33024 | tf_op jit(solution)/shard_map/psum | solution.py:140
  739.3 8.0 %copy.110 = bf16[32,128,2,512]{3,2,1,0:T(2,128)(2,1)} copy(bf16[32,128,2,512]{3,2,1,0:T(2,128)(2,1)} %collective-permute-done) | data formatting | bytes 16777216
  (62 shorter events, 6.0 us)
Async XLA Ops:
  7.2 595.5 %copy-start = (bf16[4,1024]{1,0:T(4,128)(2,1)S(1)}, bf16[4,1024]{1,0:T(4,128)(2,1)}, u32[]{:S(2)}) copy-start(bf16[4,1024]{1,0:T(4,128)(2,1)} %param.20) | copy-start | bytes 24580
  7.2 66.0 %all-gather.3.cloned.1.call-start = ((), (), s32[]{:S(2)}) async-start(), calls=%async_computation.2 | async-start | bytes 7077888 | tf_op jit(solution)/shard_map/all_gather | solution.py:69
  7.9 108.1 %copy-start.7 = (f32[2304]{0:T(1024)S(1)}, f32[2304]{0:T(1024)}, u32[]{:S(2)}) copy-start(f32[2304]{0:T(1024)} %param.17) | copy-start | bytes 27652
  7.9 108.1 %copy-start.9 = (f32[1152]{0:T(1024)S(1)}, f32[1152]{0:T(1024)}, u32[]{:S(2)}) copy-start(f32[1152]{0:T(1024)} %param.15) | copy-start | bytes 13828
  7.9 108.1 %copy-start.10 = (f32[1152]{0:T(1024)S(1)}, f32[1152]{0:T(1024)}, u32[]{:S(2)}) copy-start(f32[1152]{0:T(1024)} %param.14) | copy-start | bytes 13828
  7.9 108.1 %all-gather.5.cloned.1.call-start = ((), (), s32[]{:S(2)}) async-start(), calls=%async_computation.3 | async-start | bytes 6635520 | tf_op jit(solution)/shard_map/all_gather | solution.py:77
  8.7 351.6 %reduce-scatter.2.cloned.1.call-start = ((), (), s32[]{:S(2)}) async-start(), calls=%async_computation.4 | async-start | bytes 25165824 | tf_op jit(solution)/shard_map/reduce_scatter | solution.py:88
  73.2 3.8 copy-start.1
  78.3 62.4 %copy-start.8 = (f32[2304]{0:T(1024)S(1)}, f32[2304]{0:T(1024)}, u32[]{:S(2)}) copy-start(f32[2304]{0:T(1024)} %param.18) | copy-start | bytes 27652
  170.3 0.7 copy-start.4
  386.6 188.3 %copy-start.2 = (bf16[16,128,2,512]{3,2,1,0:T(2,128)(2,1)S(1)}, bf16[16,128,2,512]{3,2,1,0:T(2,128)(2,1)}, u32[]{:S(2)}) copy-start(bf16[16,128,2,512]{3,2,1,0:T(2,128)(2,1)} %param.21) | copy-start | bytes 12582916
  572.6 92.9 %collective-permute-start = (bf16[32,128,2,512]{3,2,1,0:T(2,128)(2,1)}, bf16[32,128,2,512]{3,2,1,0:T(2,128)(2,1)}, u32[]{:S(2)}, u32[]{:S(2)}) collective-permute-start(bf16[32,128,2,512]{3,2,1,0:T(2,128)(2,1)} %all_to_all.5), channel_id=1, source_target_pairs={{0,8},{8,16},{16,24},{24,0},{1,9},{9,17},{17,25},{25,1},{2,10},{10... | collective-permute-start | bytes 25165832 | tf_op jit(solution)/shard_map/ppermute | solution.py:18
  595.1 6.6 copy-start.5
  595.1 7.0 copy-start.11
  595.1 7.4 copy-start.6
  722.3 3.7 copy-start.3
Sparse Core Ops, SparseCore 0:
  9.6 63.6 all-gather.2
  74.8 41.2 all-gather.4
  170.4 189.8 reduce-scatter.1
where the time goes:
time: 764 us; the launch traced here: 754 us
  waiting for transfers between devices  353 us (46%)
  blocking collectives  202 us (26%)
  local copies, waits for them, and re-layouts  113 us (15%)
  matrix products  60.5 us (8%)
  between operations  14 us (2%)
  other arithmetic  10.1 us (1%)
    reduce_scatter x1, waiting for transfers between devices, per_device(): lax.psum_scatter(partial_kv, 'tp', scatter_dimension=2, tiled=True)  189 us
    all_to_all x1, blocking collectives, per_device(): lax.all_to_all(jnp.einsum('jp,ptcf->jtcf', placing, kv_pages, preferred_e...  186 us
    all_gather x1, waiting for transfers between devices, per_device(): lax.all_gather(patches, 'tp', axis=1, tiled=True).astype(jnp.float32)  64.5 us
    slice x2, local copies, waits for them, and re-layouts, attend_part(): page_store[:, :, 0, :].reshape(slot_count * page_len, head_count, HEAD_DIM)  63.1 us
    ppermute x1, waiting for transfers between devices, from_behind(): return lax.ppermute(value, axis, pairs)  60 us
    all_gather x1, waiting for transfers between devices, per_device(): lax.all_gather(w_proj, 'section', axis=0, tiled=True)  37.8 us
    dot_general x1, matrix products, per_device(): jnp.einsum('nd,dcf->ncf', hidden, w_kv, preferred_element_type=jnp.float32)  29.6 us
    dot_general x1, matrix products, per_device(): jnp.dot(x_norm, lax.all_gather(w_proj, 'section', axis=0, tiled=True), pr...  20.8 us
  transfers between devices with their start and end apart: 4, of which 4 were waited for; matrix products, arithmetic and copies ran while one was open for 5% of the time, Pallas kernels for 0%

commit v1 on v0

v1 whole, which is shorter than its diff:
```python
import jax
import jax.numpy as jnp
from jax import lax
from jax.sharding import PartitionSpec as P

HEAD_DIM = 128
IMAGE_PAGES = 32


query_scale = 1.0 / 12.0
softcap = 50.0
epsilon = 1e-06


CHUNKS = 4


def from_behind(value, axis, steps):
    count = lax.axis_size(axis)
    pairs = [(source, (source + steps) % count) for source in range(count)]
    return lax.ppermute(value, axis, pairs)


def gather_features(block):
    if lax.axis_size("tp") != 2:
        return lax.all_gather(block, "tp", axis=1, tiled=True)
    other = from_behind(block, "tp", 1)
    first = lax.axis_index("tp") == 0
    return jnp.concatenate(
        [jnp.where(first, block, other), jnp.where(first, other, block)], axis=1
    )


def sum_over_tp(value):
    if lax.axis_size("tp") != 2:
        return lax.psum(value, "tp")
    return value + from_behind(value, "tp", 1)


def columns_of(w_kv, member):
    width = w_kv.shape[2] // lax.axis_size("tp")
    part = lax.dynamic_slice_in_dim(w_kv, member * width, width, axis=2)
    return part.reshape(w_kv.shape[0], 2 * width)


def block_ranks(owners):
    per_block = owners.shape[1]
    same_owner = owners[:, :, None] == owners[:, None, :]
    earlier = jnp.arange(per_block)[None, :] < jnp.arange(per_block)[:, None]
    return jnp.sum((same_owner & earlier[None, :, :]).astype(jnp.int32), axis=2)


def attend_part(query_grid, page_store, token_mask):
    slot_count = page_store.shape[0]
    page_len = page_store.shape[1]
    head_count = page_store.shape[3] // HEAD_DIM
    keys = page_store[:, :, 0, :].reshape(slot_count * page_len, head_count, HEAD_DIM)
    values = page_store[:, :, 1, :].reshape(slot_count * page_len, head_count, HEAD_DIM)
    raw_scores = jnp.einsum("rkgd,tkd->rkgt", query_grid, keys, preferred_element_type=jnp.float32)
    capped = softcap * jnp.tanh(raw_scores * query_scale / softcap)
    allowed = token_mask.reshape(slot_count * page_len, -1).T
    weights = jnp.where(allowed[:, None, None, :], jnp.exp(capped), jnp.float32(0.0))
    totals = jnp.sum(weights, axis=3)
    weighted = jnp.einsum(
        "rkgt,tkd->rkgd", weights.astype(jnp.bfloat16), values, preferred_element_type=jnp.float32
    )
    return (totals, weighted)


def per_device(
    patches,
    vis_gain,
    vis_bias,
    w_proj,
    b_proj,
    rms_gain,
    w_kv,
    queries,
    cache,
    cache_lengths,
    slot_page,
    page_owner,
    image_request,
):
    kv_count = lax.axis_size("kv")
    section_count = lax.axis_size("section")
    section_idx = lax.axis_index("section")
    kv_idx = lax.axis_index("kv")
    row_count = patches.shape[0]
    page_len = cache.shape[1]
    pages_dev = row_count // page_len
    capacity = max(2, (2 * pages_dev + kv_count - 1) // kv_count)
    recv_slots = kv_count * capacity
    tp_count = lax.axis_size("tp")
    tp_idx = lax.axis_index("tp")
    full_w = lax.all_gather(w_proj, "section", axis=0, tiled=True)
    full_width = w_proj.shape[1] * tp_count
    w_parts = [columns_of(w_kv, (tp_idx + j) % tp_count) for j in range(tp_count)]
    tokens = page_len // CHUNKS
    patch_pages = patches.reshape(pages_dev, page_len, -1)
    own_owners = lax.dynamic_index_in_dim(page_owner, section_idx, 0, keepdims=False).reshape(
        kv_count, pages_dev
    )
    my_owner = lax.dynamic_index_in_dim(own_owners, kv_idx, 0, keepdims=False)
    my_rank = lax.dynamic_index_in_dim(block_ranks(own_owners), kv_idx, 0, keepdims=False)
    new_pages = jnp.zeros((recv_slots, page_len, 2, cache.shape[3]), jnp.bfloat16)
    handed_parts = []
    for c in range(CHUNKS):
        block = patch_pages[:, c * tokens : (c + 1) * tokens, :].reshape(pages_dev * tokens, -1)
        gathered = gather_features(block).astype(jnp.float32)
        row_mean = jnp.mean(gathered, axis=1, keepdims=True)
        centred = gathered - row_mean
        variance = jnp.mean(centred * centred, axis=1, keepdims=True)
        x_norm = (centred * lax.rsqrt(variance + epsilon) * vis_gain + vis_bias).astype(
            jnp.bfloat16
        )
        projected = jnp.dot(x_norm, full_w, preferred_element_type=jnp.float32) + b_proj
        squares = sum_over_tp(jnp.sum(projected * projected, axis=1))
        hidden = (
            projected * lax.rsqrt(squares / full_width + epsilon)[:, None] * rms_gain
        ).astype(jnp.bfloat16)
        arrived = [
            from_behind(
                jnp.dot(hidden, w_parts[j], preferred_element_type=jnp.float32).astype(
                    jnp.bfloat16
                ),
                "tp",
                j,
            )
            for j in range(1, tp_count)
        ]
        image_kv = jnp.dot(hidden, w_parts[0], preferred_element_type=jnp.float32)
        for part in arrived:
            image_kv = image_kv + part.astype(jnp.float32)
        handed = from_behind(
            image_kv.astype(jnp.bfloat16).reshape(pages_dev, tokens, -1), "section", 1
        )
        handed_parts.append(handed)
        for j in range(kv_count):
            owner = (kv_idx + j) % kv_count
            placing = (
                (jnp.arange(capacity)[:, None] == my_rank[None, :]) & (my_owner == owner)[None, :]
            ).astype(jnp.bfloat16)
            outgoing = jnp.einsum(
                "jp,ptf->jtf", placing, handed, preferred_element_type=jnp.float32
            ).astype(jnp.bfloat16)
            incoming = from_behind(outgoing, "kv", j) if j else outgoing
            source = (kv_idx - j) % kv_count
            new_pages = lax.dynamic_update_slice(
                new_pages,
                incoming.reshape(capacity, tokens, 2, -1),
                (source * capacity, c * tokens, 0, 0),
            )
    req_count = queries.shape[0]
    kv_heads_dev = cache.shape[3] // HEAD_DIM
    group_size = queries.shape[1] // HEAD_DIM // kv_heads_dev
    query_grid = queries.reshape(req_count, kv_heads_dev, group_size, HEAD_DIM)
    lengths = cache_lengths[0]
    page_counts = (lengths + page_len - 1) // page_len
    starts = jnp.cumsum(page_counts) - page_counts
    slot_ids = slot_page[0]
    within = slot_ids[:, None] - starts[None, :]
    inside = (within >= 0) & (within < page_counts[None, :])
    valid = jnp.where(inside, jnp.clip(lengths[None, :] - within * page_len, 0, page_len), 0)
    cache_mask = jnp.arange(page_len)[None, :, None] < valid[:, None, :]
    cache_totals, cache_weighted = attend_part(query_grid, cache, cache_mask)
    image_of = (kv_idx * pages_dev + jnp.arange(pages_dev)) // IMAGE_PAGES
    image_hit = image_of[:, None] == jnp.arange(image_request.shape[1])[None, :]
    page_request = jnp.sum(jnp.where(image_hit, image_request[0][None, :], 0), axis=1)
    request_hit = page_request[:, None] == jnp.arange(req_count)[None, :]
    handed_mask = jnp.broadcast_to(request_hit[:, None, :], (pages_dev, tokens, req_count))
    totals, weighted = cache_totals, cache_weighted
    for handed in handed_parts:
        part_totals, part_weighted = attend_part(
            query_grid, handed.reshape(pages_dev, tokens, 2, -1), handed_mask
        )
        totals, weighted = totals + part_totals, weighted + part_weighted
    totals, weighted = lax.psum((totals, weighted), "kv")
    attended = (weighted / totals[..., None]).astype(jnp.bfloat16).reshape(req_count, -1)
    return (new_pages, attended)


def solution(mesh):
    in_specs = (
        P(("section", "kv"), "tp"),
        P(),
        P(),
        P("section", "tp"),
        P("tp"),
        P("tp"),
        P("tp", None, None),
        P("section", "tp"),
        P(("section", "kv"), None, None, "tp"),
        P("section", None),
        P("section", "kv"),
        P(),
        P("section", None),
    )
    out_specs = (P(("section", "kv"), None, None, "tp"), P("section", "tp"))
    return jax.shard_map(
        per_device, mesh=mesh, in_specs=in_specs, out_specs=out_specs, check_vma=False
    )
```

time: 764 us -> 482 us (0.63)
  waiting for transfers between devices: 353 us -> 114 us
  blocking collectives: 202 us -> 59.1 us
  starting transfers between devices: 2.34 us -> 55.5 us
  local copies, waits for them, and re-layouts: 113 us -> 154 us
    reduce_scatter x1 -> x0, waiting for transfers between devices: 189 us -> none  [per_device(): lax.psum_scatter(partial_kv, 'tp', scatter_dimension=2, tiled=True)]
    all_to_all x1 -> x0, blocking collectives: 186 us -> none  [per_device(): lax.all_to_all(jnp.einsum('jp,ptcf->jtcf', placing, kv_pages, preferred_e...]
    all_gather x2 -> x1, waiting for transfers between devices: 102 us -> 0.02 us  [per_device(): full_w = lax.all_gather(w_proj, 'section', axis=0, tiled=True)]
    ppermute x1 -> x28, waiting for transfers between devices: 60 us -> 114 us  [from_behind(): return lax.ppermute(value, axis, pairs)]
    ppermute x1 -> x28, starting transfers between devices: 2.23 us -> 55.5 us  [from_behind(): return lax.ppermute(value, axis, pairs)]
    psum x2 -> x1, blocking collectives: 15.8 us -> 59.1 us  [per_device(): totals, weighted = lax.psum((totals, weighted), 'kv')]
    dynamic_update_slice x0 -> x16, local copies, waits for them, and re-layouts: none -> 24.4 us  [per_device(): lax.dynamic_update_slice(new_pages, incoming.reshape(capacity, tokens, 2,...]
    slice x2 -> x5, local copies, waits for them, and re-layouts: 63.1 us -> 39.7 us  [attend_part(): page_store[:, :, 0, :].reshape(slot_count * page_len, head_count, HEAD_DIM)]
  transfers between devices with their start and end apart: 4 -> 29, of which waited for: 4 -> 7; matrix products, arithmetic and copies ran while one was open for 5% -> 38% of each run, Pallas kernels for 0% -> 0%
where the time goes in v1:
time: 482 us; the launch traced here: 473 us
  local copies, waits for them, and re-layouts  154 us (32%)
  waiting for transfers between devices  114 us (24%)
  matrix products  67.7 us (14%)
  blocking collectives  59.1 us (12%)
  starting transfers between devices  55.5 us (12%)
  between operations  15.1 us (3%)
  other arithmetic  8.07 us (2%)
    ppermute x28, waiting for transfers between devices, from_behind(): return lax.ppermute(value, axis, pairs)  114 us
    psum x1, blocking collectives, per_device(): totals, weighted = lax.psum((totals, weighted), 'kv')  59.1 us
    ppermute x28, starting transfers between devices, from_behind(): return lax.ppermute(value, axis, pairs)  55.5 us
    slice x5, local copies, waits for them, and re-layouts, attend_part(): page_store[:, :, 0, :].reshape(slot_count * page_len, head_count, HEAD_DIM)  39.7 us
    dynamic_update_slice x16, local copies, waits for them, and re-layouts, per_device(): lax.dynamic_update_slice(new_pages, incoming.reshape(capacity, tokens, 2,...  24.4 us
    unnamed x81, local copies, waits for them, and re-layouts  23.6 us
    dot_general x16, matrix products, per_device(): jnp.einsum('jp,ptf->jtf', placing, handed, preferred_element_type=jnp.flo...  18.4 us
    dot_general x4, matrix products, per_device(): jnp.dot(x_norm, full_w, preferred_element_type=jnp.float32) + b_proj  17.9 us
  transfers between devices with their start and end apart: 29, of which 7 were waited for; matrix products, arithmetic and copies ran while one was open for 38% of the time, Pallas kernels for 0%

profile of v1, /device:TPU:25, one launch (start us, length us, event | category | flops | bytes accessed | tf_op | source)
XLA Modules:
  0.0 473.0 jit_solution(17881327186296622052)
XLA Ops:
  20.2 8.0 %constant_dynamic-slice_fusion.1 = (bf16[2304,2,512]{2,1,0:T(2,128)(2,1)S(1)}, bf16[2304,2,512]{2,1,0:T(2,128)(2,1)S(1)}) fusion(bf16[2304,2,1024]{2,1,0:T(2,128)(2,1)} %param.19, s32[]{:T(128)S(6)} %select_n.220, s32[]{:T(128)S(6)} %select_n.222), kind=kLoop, calls=%fused_computation.177 | loop fusion | bytes 18874376 | tf_op jit(solution)/shard_map/dynamic_slice | solution.py:42
  28.2 3.7 copy.255
  31.9 3.7 copy.254
  35.9 21.9 %slice_reduce_fusion.1 = (bf16[16,128,512]{2,1,0:T(8,128)(2,1)}, bf16[16,128,512]{2,1,0:T(8,128)(2,1)S(1)}) fusion(bf16[16,128,2,512]{3,2,1,0:T(2,128)(2,1)} %param.21), kind=kLoop, calls=%fused_computation.13 | loop fusion | bytes 8388608 | tf_op jit(solution)/shard_map/slice | solution.py:57
  57.8 4.0 reshape.354
  82.3 6.7 %multiply_reduce_fusion = (f32[512]{0:T(512)S(1)}, f32[512,2304]{1,0:T(8,128)S(1)}) fusion(f32[2304]{0:T(1024)S(1)} %copy-done.26, bf16[1152,2304]{1,0:T(8,128)(2,1)} %all-gather.2.cloned.1.call-done, f32[512]{0:T(512)S(1)} %add_rsqrt_fusion.1, f32[512]{0:T(512)S(1)} %broadcast_multiply_fusion, f32[1152]{0:T(1024)S(1)} %copy-done.28, ...), kind=kOutput, calls=%fused_computation.5 | convolution fusion | flops 2726755840 | bytes 11231232 | tf_op jit(solution)/shard_map/dot_general | solution.py:117
  90.2 3.9 multiply_reduce_fusion.1
  118.0 9.9 %collective-permute-done.23 = bf16[512,1024]{1,0:T(8,128)(2,1)S(1)} collective-permute-done((bf16[512,1024]{1,0:T(8,128)(2,1)S(1)}, bf16[512,1024]{1,0:T(8,128)(2,1)S(1)}, u32[]{:S(2)}, u32[]{:S(2)}) %collective-permute-start.23) | collective-permute-done | bytes 1048608 | tf_op jit(solution)/shard_map/ppermute | solution.py:21
  131.3 8.6 %collective-permute-start.24 = (bf16[16,32,1024]{2,0,1:T(8,128)(2,1)S(1)}, bf16[16,32,1024]{2,0,1:T(8,128)(2,1)S(1)}, u32[]{:S(2)}, u32[]{:S(2)}) collective-permute-start(bf16[16,32,1024]{2,0,1:T(8,128)(2,1)S(1)} %copy.181), channel_id=1, source_target_pairs={{0,8},{8,16},{16,24},{24,0},{1,9},{9,17},{17,25},{25,1},{2,10},{10... | collective-permute-start | bytes 3145736 | tf_op jit(solution)/shard_map/ppermute | solution.py:21
  139.9 10.5 %collective-permute-done.16 = bf16[512,1024]{1,0:T(8,128)(2,1)S(1)} collective-permute-done((bf16[512,1024]{1,0:T(8,128)(2,1)S(1)}, bf16[512,1024]{1,0:T(8,128)(2,1)S(1)}, u32[]{:S(2)}, u32[]{:S(2)}) %collective-permute-start.16) | collective-permute-done | bytes 1048608 | tf_op jit(solution)/shard_map/ppermute | solution.py:21
  154.7 8.6 %collective-permute-start.17 = (bf16[16,32,1024]{2,0,1:T(8,128)(2,1)}, bf16[16,32,1024]{2,0,1:T(8,128)(2,1)S(1)}, u32[]{:S(2)}, u32[]{:S(2)}) collective-permute-start(bf16[16,32,1024]{2,0,1:T(8,128)(2,1)} %copy.172), channel_id=1, source_target_pairs={{0,8},{8,16},{16,24},{24,0},{1,9},{9,17},{17,25},{25,1},{2,10},{10... | collective-permute-start | bytes 3145736 | tf_op jit(solution)/shard_map/ppermute | solution.py:21
  163.3 9.6 %collective-permute-done.9 = bf16[512,1024]{1,0:T(8,128)(2,1)S(1)} collective-permute-done((bf16[512,1024]{1,0:T(8,128)(2,1)S(1)}, bf16[512,1024]{1,0:T(8,128)(2,1)S(1)}, u32[]{:S(2)}, u32[]{:S(2)}) %collective-permute-start.9) | collective-permute-done | bytes 1048608 | tf_op jit(solution)/shard_map/ppermute | solution.py:21
  177.2 8.7 %collective-permute-start.10 = (bf16[16,32,1024]{2,0,1:T(8,128)(2,1)}, bf16[16,32,1024]{2,0,1:T(8,128)(2,1)S(1)}, u32[]{:S(2)}, u32[]{:S(2)}) collective-permute-start(bf16[16,32,1024]{2,0,1:T(8,128)(2,1)} %copy.163), channel_id=1, source_target_pairs={{0,8},{8,16},{16,24},{24,0},{1,9},{9,17},{17,25},{25,1},{2,10},{10... | collective-permute-start | bytes 3145736 | tf_op jit(solution)/shard_map/ppermute | solution.py:21
  185.9 9.4 %collective-permute-done.2 = bf16[512,1024]{1,0:T(8,128)(2,1)S(1)} collective-permute-done((bf16[512,1024]{1,0:T(8,128)(2,1)S(1)}, bf16[512,1024]{1,0:T(8,128)(2,1)S(1)}, u32[]{:S(2)}, u32[]{:S(2)}) %collective-permute-start.2) | collective-permute-done | bytes 1048608 | tf_op jit(solution)/shard_map/ppermute | solution.py:21
  199.6 5.0 %collective-permute-start.3 = (bf16[16,32,1024]{2,0,1:T(8,128)(2,1)}, bf16[16,32,1024]{2,0,1:T(8,128)(2,1)}, u32[]{:S(2)}, u32[]{:S(2)}) collective-permute-start(bf16[16,32,1024]{2,0,1:T(8,128)(2,1)} %copy.154), channel_id=1, source_target_pairs={{0,8},{8,16},{16,24},{24,0},{1,9},{9,17},{17,25},{25,1},{2,10},{10... | collective-permute-start | bytes 3145736 | tf_op jit(solution)/shard_map/ppermute | solution.py:21
  206.2 4.4 fusion.144
  215.5 4.4 fusion.143
  224.8 4.4 fusion.142
  239.3 4.6 fusion.141
  291.2 5.4 %broadcast_in_dim.43 = bf16[32,128,2,512]{3,2,1,0:T(2,128)(2,1)} broadcast(bf16[]{:T(256)} %constant.191.clone.1), dimensions={} | broadcast | bytes 8388610 | tf_op jit(solution)/shard_map/broadcast_in_dim | solution.py:106
  297.8 59.1 %all-reduce = (f32[4,4,2,128]{3,0,2,1:T(4,128)S(1)}, f32[4,4,2]{0,2,1:T(2,128)S(1)}) all-reduce(f32[4,4,2,128]{3,0,2,1:T(4,128)S(1)} %fusion.84, f32[4,4,2]{0,2,1:T(2,128)S(1)} %bitcast.280), channel_id=1, replica_groups=mesh['section'=4,'kv'=4,'tp'=2] {'kv'}, use_global_device_ids=true, to_apply=%region_15.16 | all-reduce | flops 4128 | bytes 33024 | tf_op jit(solution)/shard_map/psum | solution.py:178
  379.7 4.9 %collective-permute-done.18 = bf16[8,32,1024]{2,0,1:T(8,128)(2,1)S(1)} collective-permute-done((bf16[8,32,1024]{2,0,1:T(8,128)(2,1)}, bf16[8,32,1024]{2,0,1:T(8,128)(2,1)S(1)}, u32[]{:S(2)}, u32[]{:S(2)}) %collective-permute-start.18) | collective-permute-done | bytes 524320 | tf_op jit(solution)/shard_map/ppermute | solution.py:21
  389.1 32.2 %collective-permute-done.19 = bf16[8,32,1024]{2,0,1:T(8,128)(2,1)S(1)} collective-permute-done((bf16[8,32,1024]{2,0,1:T(8,128)(2,1)S(1)}, bf16[8,32,1024]{2,0,1:T(8,128)(2,1)S(1)}, u32[]{:S(2)}, u32[]{:S(2)}) %collective-permute-start.19) | collective-permute-done | bytes 524320 | tf_op jit(solution)/shard_map/ppermute | solution.py:21
  426.1 37.2 %collective-permute-done.26 = bf16[8,32,1024]{2,0,1:T(8,128)(2,1)S(1)} collective-permute-done((bf16[8,32,1024]{2,0,1:T(8,128)(2,1)S(1)}, bf16[8,32,1024]{2,0,1:T(8,128)(2,1)S(1)}, u32[]{:S(2)}, u32[]{:S(2)}) %collective-permute-start.26) | collective-permute-done | bytes 524320 | tf_op jit(solution)/shard_map/ppermute | solution.py:21
  (253 shorter events, 179.2 us)
Async XLA Ops:
  7.2 75.0 %all-gather.2.cloned.1.call-start = ((), (), s32[]{:S(2)}) async-start(), calls=%async_computation | async-start | bytes 6635520 | tf_op jit(solution)/shard_map/all_gather | solution.py:96
  14.0 53.8 %collective-permute-start.21 = (bf16[512,576]{0,1:T(8,128)(2,1)}, bf16[512,576]{0,1:T(8,128)(2,1)}, u32[]{:S(2)}, u32[]{:S(2)}) collective-permute-start(bf16[512,576]{0,1:T(8,128)(2,1)} %copy.178), channel_id=1, source_target_pairs={{0,1},{1,0},{2,3},{3,2},{4,5},{5,4},{6,7},{7,6},{8,9},{9,8},{10,11... | collective-permute-start | bytes 1769480 | tf_op jit(solution)/shard_map/ppermute | solution.py:21
  16.3 52.9 %collective-permute-start.14 = (bf16[512,576]{0,1:T(8,128)(2,1)}, bf16[512,576]{0,1:T(8,128)(2,1)}, u32[]{:S(2)}, u32[]{:S(2)}) collective-permute-start(bf16[512,576]{0,1:T(8,128)(2,1)} %copy.169), channel_id=1, source_target_pairs={{0,1},{1,0},{2,3},{3,2},{4,5},{5,4},{6,7},{7,6},{8,9},{9,8},{10,11... | collective-permute-start | bytes 1769480 | tf_op jit(solution)/shard_map/ppermute | solution.py:21
  17.6 53.0 %collective-permute-start.7 = (bf16[512,576]{0,1:T(8,128)(2,1)}, bf16[512,576]{0,1:T(8,128)(2,1)}, u32[]{:S(2)}, u32[]{:S(2)}) collective-permute-start(bf16[512,576]{0,1:T(8,128)(2,1)} %copy.160), channel_id=1, source_target_pairs={{0,1},{1,0},{2,3},{3,2},{4,5},{5,4},{6,7},{7,6},{8,9},{9,8},{10,11... | collective-permute-start | bytes 1769480 | tf_op jit(solution)/shard_map/ppermute | solution.py:21
  19.9 52.9 %collective-permute-start = (bf16[512,576]{0,1:T(8,128)(2,1)}, bf16[512,576]{0,1:T(8,128)(2,1)}, u32[]{:S(2)}, u32[]{:S(2)}) collective-permute-start(bf16[512,576]{0,1:T(8,128)(2,1)} %copy.151), channel_id=1, source_target_pairs={{0,1},{1,0},{2,3},{3,2},{4,5},{5,4},{6,7},{7,6},{8,9},{9,8},{10,11... | collective-permute-start | bytes 1769480 | tf_op jit(solution)/shard_map/ppermute | solution.py:21
  106.2 21.7 %collective-permute-start.23 = (bf16[512,1024]{1,0:T(8,128)(2,1)S(1)}, bf16[512,1024]{1,0:T(8,128)(2,1)S(1)}, u32[]{:S(2)}, u32[]{:S(2)}) collective-permute-start(bf16[512,1024]{1,0:T(8,128)(2,1)S(1)} %convolution_convert_fusion), channel_id=1, source_target_pairs={{0,1},{1,0},{2,3},{3,2},{4,5},{5,4},{6,7},{7,6},{8,9},{9,8},{10,11... | collective-permute-start | bytes 3145736 | tf_op jit(solution)/shard_map/ppermute | solution.py:21
  110.6 39.8 %collective-permute-start.16 = (bf16[512,1024]{1,0:T(8,128)(2,1)S(1)}, bf16[512,1024]{1,0:T(8,128)(2,1)S(1)}, u32[]{:S(2)}, u32[]{:S(2)}) collective-permute-start(bf16[512,1024]{1,0:T(8,128)(2,1)S(1)} %convolution_convert_fusion.1), channel_id=1, source_target_pairs={{0,1},{1,0},{2,3},{3,2},{4,5},{5,4},{6,7},{7,6},{8,9},{9,8},{10,11... | collective-permute-start | bytes 3145736 | tf_op jit(solution)/shard_map/ppermute | solution.py:21
  113.7 59.2 %collective-permute-start.9 = (bf16[512,1024]{1,0:T(8,128)(2,1)S(1)}, bf16[512,1024]{1,0:T(8,128)(2,1)S(1)}, u32[]{:S(2)}, u32[]{:S(2)}) collective-permute-start(bf16[512,1024]{1,0:T(8,128)(2,1)S(1)} %convolution_convert_fusion.2), channel_id=1, source_target_pairs={{0,1},{1,0},{2,3},{3,2},{4,5},{5,4},{6,7},{7,6},{8,9},{9,8},{10,11... | collective-permute-start | bytes 3145736 | tf_op jit(solution)/shard_map/ppermute | solution.py:21
  117.7 77.6 %collective-permute-start.2 = (bf16[512,1024]{1,0:T(8,128)(2,1)S(1)}, bf16[512,1024]{1,0:T(8,128)(2,1)S(1)}, u32[]{:S(2)}, u32[]{:S(2)}) collective-permute-start(bf16[512,1024]{1,0:T(8,128)(2,1)S(1)} %convolution_convert_fusion.3), channel_id=1, source_target_pairs={{0,1},{1,0},{2,3},{3,2},{4,5},{5,4},{6,7},{7,6},{8,9},{9,8},{10,11... | collective-permute-start | bytes 3145736 | tf_op jit(solution)/shard_map/ppermute | solution.py:21
  131.3 73.4 %collective-permute-start.24 = (bf16[16,32,1024]{2,0,1:T(8,128)(2,1)S(1)}, bf16[16,32,1024]{2,0,1:T(8,128)(2,1)S(1)}, u32[]{:S(2)}, u32[]{:S(2)}) collective-permute-start(bf16[16,32,1024]{2,0,1:T(8,128)(2,1)S(1)} %copy.181), channel_id=1, source_target_pairs={{0,8},{8,16},{16,24},{24,0},{1,9},{9,17},{17,25},{25,1},{2,10},{10... | collective-permute-start | bytes 3145736 | tf_op jit(solution)/shard_map/ppermute | solution.py:21
  154.7 59.3 %collective-permute-start.17 = (bf16[16,32,1024]{2,0,1:T(8,128)(2,1)}, bf16[16,32,1024]{2,0,1:T(8,128)(2,1)S(1)}, u32[]{:S(2)}, u32[]{:S(2)}) collective-permute-start(bf16[16,32,1024]{2,0,1:T(8,128)(2,1)} %copy.172), channel_id=1, source_target_pairs={{0,8},{8,16},{16,24},{24,0},{1,9},{9,17},{17,25},{25,1},{2,10},{10... | collective-permute-start | bytes 3145736 | tf_op jit(solution)/shard_map/ppermute | solution.py:21
  177.2 46.1 %collective-permute-start.10 = (bf16[16,32,1024]{2,0,1:T(8,128)(2,1)}, bf16[16,32,1024]{2,0,1:T(8,128)(2,1)S(1)}, u32[]{:S(2)}, u32[]{:S(2)}) collective-permute-start(bf16[16,32,1024]{2,0,1:T(8,128)(2,1)} %copy.163), channel_id=1, source_target_pairs={{0,8},{8,16},{16,24},{24,0},{1,9},{9,17},{17,25},{25,1},{2,10},{10... | collective-permute-start | bytes 3145736 | tf_op jit(solution)/shard_map/ppermute | solution.py:21
  199.6 37.1 %collective-permute-start.3 = (bf16[16,32,1024]{2,0,1:T(8,128)(2,1)}, bf16[16,32,1024]{2,0,1:T(8,128)(2,1)}, u32[]{:S(2)}, u32[]{:S(2)}) collective-permute-start(bf16[16,32,1024]{2,0,1:T(8,128)(2,1)} %copy.154), channel_id=1, source_target_pairs={{0,8},{8,16},{16,24},{24,0},{1,9},{9,17},{17,25},{25,1},{2,10},{10... | collective-permute-start | bytes 3145736 | tf_op jit(solution)/shard_map/ppermute | solution.py:21
  269.2 88.4 %collective-permute-start.4 = (bf16[8,32,1024]{2,0,1:T(8,128)(2,1)}, bf16[8,32,1024]{2,0,1:T(8,128)(2,1)}, u32[]{:S(2)}, u32[]{:S(2)}) collective-permute-start(bf16[8,32,1024]{2,0,1:T(8,128)(2,1)} %convolution_convert_fusion.18), channel_id=1, source_target_pairs={{0,2},{2,4},{4,6},{6,0},{1,3},{3,5},{5,7},{7,1},{8,10},{10,12},{12... | collective-permute-start | bytes 1572872 | tf_op jit(solution)/shard_map/ppermute | solution.py:21
  271.5 88.3 %collective-permute-start.5 = (bf16[8,32,1024]{2,0,1:T(8,128)(2,1)}, bf16[8,32,1024]{2,0,1:T(8,128)(2,1)}, u32[]{:S(2)}, u32[]{:S(2)}) collective-permute-start(bf16[8,32,1024]{2,0,1:T(8,128)(2,1)} %convolution_convert_fusion.17), channel_id=1, source_target_pairs={{0,4},{2,6},{4,0},{6,2},{1,5},{3,7},{5,1},{7,3},{8,12},{10,14},{12... | collective-permute-start | bytes 1572872 | tf_op jit(solution)/shard_map/ppermute | solution.py:21
  275.3 90.3 %collective-permute-start.6 = (bf16[8,32,1024]{2,0,1:T(8,128)(2,1)}, bf16[8,32,1024]{2,0,1:T(8,128)(2,1)}, u32[]{:S(2)}, u32[]{:S(2)}) collective-permute-start(bf16[8,32,1024]{2,0,1:T(8,128)(2,1)} %convolution_convert_fusion.16), channel_id=1, source_target_pairs={{0,6},{2,0},{4,2},{6,4},{1,7},{3,1},{5,3},{7,5},{8,14},{10,8},{12,... | collective-permute-start | bytes 1572872 | tf_op jit(solution)/shard_map/ppermute | solution.py:21
  276.5 92.5 %collective-permute-start.11 = (bf16[8,32,1024]{2,0,1:T(8,128)(2,1)}, bf16[8,32,1024]{2,0,1:T(8,128)(2,1)}, u32[]{:S(2)}, u32[]{:S(2)}) collective-permute-start(bf16[8,32,1024]{2,0,1:T(8,128)(2,1)} %convolution_convert_fusion.14), channel_id=1, source_target_pairs={{0,2},{2,4},{4,6},{6,0},{1,3},{3,5},{5,7},{7,1},{8,10},{10,12},{12... | collective-permute-start | bytes 1572872 | tf_op jit(solution)/shard_map/ppermute | solution.py:21
  280.7 90.9 %collective-permute-start.12 = (bf16[8,32,1024]{2,0,1:T(8,128)(2,1)}, bf16[8,32,1024]{2,0,1:T(8,128)(2,1)}, u32[]{:S(2)}, u32[]{:S(2)}) collective-permute-start(bf16[8,32,1024]{2,0,1:T(8,128)(2,1)} %convolution_convert_fusion.13), channel_id=1, source_target_pairs={{0,4},{2,6},{4,0},{6,2},{1,5},{3,7},{5,1},{7,3},{8,12},{10,14},{12... | collective-permute-start | bytes 1572872 | tf_op jit(solution)/shard_map/ppermute | solution.py:21
  359.8 24.8 %collective-permute-start.18 = (bf16[8,32,1024]{2,0,1:T(8,128)(2,1)}, bf16[8,32,1024]{2,0,1:T(8,128)(2,1)S(1)}, u32[]{:S(2)}, u32[]{:S(2)}) collective-permute-start(bf16[8,32,1024]{2,0,1:T(8,128)(2,1)} %convolution_convert_fusion.10), channel_id=1, source_target_pairs={{0,2},{2,4},{4,6},{6,0},{1,3},{3,5},{5,7},{7,1},{8,10},{10,12},{12... | collective-permute-start | bytes 1572872 | tf_op jit(solution)/shard_map/ppermute | solution.py:21
  365.6 55.8 %collective-permute-start.19 = (bf16[8,32,1024]{2,0,1:T(8,128)(2,1)S(1)}, bf16[8,32,1024]{2,0,1:T(8,128)(2,1)S(1)}, u32[]{:S(2)}, u32[]{:S(2)}) collective-permute-start(bf16[8,32,1024]{2,0,1:T(8,128)(2,1)S(1)} %copy-done.22), channel_id=1, source_target_pairs={{0,4},{2,6},{4,0},{6,2},{1,5},{3,7},{5,1},{7,3},{8,12},{10,14},{12... | collective-permute-start | bytes 1572872 | tf_op jit(solution)/shard_map/ppermute | solution.py:21
  369.0 53.5 %collective-permute-start.20 = (bf16[8,32,1024]{2,0,1:T(8,128)(2,1)S(1)}, bf16[8,32,1024]{2,0,1:T(8,128)(2,1)S(1)}, u32[]{:S(2)}, u32[]{:S(2)}) collective-permute-start(bf16[8,32,1024]{2,0,1:T(8,128)(2,1)S(1)} %convolution_convert_fusion.8), channel_id=1, source_target_pairs={{0,6},{2,0},{4,2},{6,4},{1,7},{3,1},{5,3},{7,5},{8,14},{10,8},{12,... | collective-permute-start | bytes 1572872 | tf_op jit(solution)/shard_map/ppermute | solution.py:21
  371.6 53.4 %collective-permute-start.25 = (bf16[8,32,1024]{2,0,1:T(8,128)(2,1)S(1)}, bf16[8,32,1024]{2,0,1:T(8,128)(2,1)S(1)}, u32[]{:S(2)}, u32[]{:S(2)}) collective-permute-start(bf16[8,32,1024]{2,0,1:T(8,128)(2,1)S(1)} %convolution_convert_fusion.6), channel_id=1, source_target_pairs={{0,2},{2,4},{4,6},{6,0},{1,3},{3,5},{5,7},{7,1},{8,10},{10,12},{12... | collective-permute-start | bytes 1572872 | tf_op jit(solution)/shard_map/ppermute | solution.py:21
  376.8 86.5 %collective-permute-start.26 = (bf16[8,32,1024]{2,0,1:T(8,128)(2,1)S(1)}, bf16[8,32,1024]{2,0,1:T(8,128)(2,1)S(1)}, u32[]{:S(2)}, u32[]{:S(2)}) collective-permute-start(bf16[8,32,1024]{2,0,1:T(8,128)(2,1)S(1)} %convolution_convert_fusion.5), channel_id=1, source_target_pairs={{0,4},{2,6},{4,0},{6,2},{1,5},{3,7},{5,1},{7,3},{8,12},{10,14},{12... | collective-permute-start | bytes 1572872 | tf_op jit(solution)/shard_map/ppermute | solution.py:21
  384.6 79.9 %collective-permute-start.27 = (bf16[8,32,1024]{2,0,1:T(8,128)(2,1)S(1)}, bf16[8,32,1024]{2,0,1:T(8,128)(2,1)S(1)}, u32[]{:S(2)}, u32[]{:S(2)}) collective-permute-start(bf16[8,32,1024]{2,0,1:T(8,128)(2,1)S(1)} %convolution_convert_fusion.4), channel_id=1, source_target_pairs={{0,6},{2,0},{4,2},{6,4},{1,7},{3,1},{5,3},{7,5},{8,14},{10,8},{12,... | collective-permute-start | bytes 1572872 | tf_op jit(solution)/shard_map/ppermute | solution.py:21
  (40 other events, 489.0 us)
Sparse Core Ops, SparseCore 0:
  15.3 41.5 all-gather.1

commit v2 on v1

--- a/solution.py
+++ b/solution.py
@@ -1,6 +1,8 @@
 import jax
 import jax.numpy as jnp
 from jax import lax
+from jax.experimental import pallas as pl
+from jax.experimental.pallas import tpu as pltpu
 from jax.sharding import PartitionSpec as P
 
 HEAD_DIM = 128
@@ -50,21 +52,60 @@
     return jnp.sum((same_owner & earlier[None, :, :]).astype(jnp.int32), axis=2)
 
 
-def attend_part(query_grid, page_store, token_mask):
-    slot_count = page_store.shape[0]
-    page_len = page_store.shape[1]
-    head_count = page_store.shape[3] // HEAD_DIM
-    keys = page_store[:, :, 0, :].reshape(slot_count * page_len, head_count, HEAD_DIM)
-    values = page_store[:, :, 1, :].reshape(slot_count * page_len, head_count, HEAD_DIM)
-    raw_scores = jnp.einsum("rkgd,tkd->rkgt", query_grid, keys, preferred_element_type=jnp.float32)
-    capped = softcap * jnp.tanh(raw_scores * query_scale / softcap)
-    allowed = token_mask.reshape(slot_count * page_len, -1).T
-    weights = jnp.where(allowed[:, None, None, :], jnp.exp(capped), jnp.float32(0.0))
-    totals = jnp.sum(weights, axis=3)
-    weighted = jnp.einsum(
-        "rkgt,tkd->rkgd", weights.astype(jnp.bfloat16), values, preferred_element_type=jnp.float32
-    )
-    return (totals, weighted)
+def attend_kernel(head_count, parts, query_ref, *refs):
+    masks, stores = refs[:parts], refs[parts : 2 * parts]
+    totals_ref, weighted_ref = refs[2 * parts :]
+    half = head_count * HEAD_DIM
+    for k in range(head_count):
+        query = query_ref[k]
+        total = jnp.zeros((query.shape[0], 1), jnp.float32)
+        numer = jnp.zeros((query.shape[0], HEAD_DIM), jnp.float32)
+        for mask_ref, store_ref in zip(masks, stores):
+            keys = store_ref[:, k * HEAD_DIM : (k + 1) * HEAD_DIM]
+            values = store_ref[:, half + k * HEAD_DIM : half + (k + 1) * HEAD_DIM]
+            raw = lax.dot_general(
+                query, keys, (((1,), (1,)), ((), ())), preferred_element_type=jnp.float32
+            )
+            capped = softcap * jnp.tanh(raw * query_scale / softcap)
+            weights = jnp.where(mask_ref[...] > 0.0, jnp.exp(capped), jnp.float32(0.0))
+            total = total + jnp.sum(weights, axis=1, keepdims=True)
+            numer = numer + jnp.dot(
+                weights.astype(jnp.bfloat16), values, preferred_element_type=jnp.float32
+            )
+        totals_ref[k] = jnp.broadcast_to(total, numer.shape)
+        weighted_ref[k] = numer
+
+
+def attend_all(query_grid, masks, stores):
+    head_count, rows = query_grid.shape[:2]
+    tokens = sum(store.shape[0] for store in stores)
+    result = jax.ShapeDtypeStruct((head_count, rows, HEAD_DIM), jnp.float32)
+    return pl.pallas_call(
+        lambda *refs: attend_kernel(head_count, len(stores), *refs),
+        out_shape=(result, result),
+        in_specs=[pl.BlockSpec(memory_space=pltpu.VMEM)] * (1 + 2 * len(stores)),
+        out_specs=(pl.BlockSpec(memory_space=pltpu.VMEM),) * 2,
+        compiler_params=pltpu.CompilerParams(vmem_limit_bytes=40 * 1024 * 1024),
+        cost_estimate=pl.CostEstimate(
+            flops=4 * tokens * head_count * rows * HEAD_DIM * 8,
+            bytes_accessed=4 * tokens * head_count * HEAD_DIM,
+            transcendentals=2 * tokens * head_count * rows,
+        ),
+    )(query_grid, *masks, *stores)
+
+
+def sum_over_kv(value):
+    count = lax.axis_size("kv")
+    if count > 4:
+        return lax.psum(value, "kv")
+    here = lax.axis_index("kv")
+    shifted = jnp.stack([from_behind(value, "kv", j) if j else value for j in range(count)])
+    total = jnp.zeros_like(value)
+    for source in range(count):
+        total = total + lax.dynamic_index_in_dim(
+            shifted, (here - source + count) % count, 0, keepdims=False
+        )
+    return total
 
 
 def per_device(
@@ -105,6 +146,19 @@
     my_rank = lax.dynamic_index_in_dim(block_ranks(own_owners), kv_idx, 0, keepdims=False)
     new_pages = jnp.zeros((recv_slots, page_len, 2, cache.shape[3]), jnp.bfloat16)
     handed_parts = []
+    outgoing_all = []
+
+    def exchange(pages, blocks, c):
+        for j in range(kv_count):
+            incoming = from_behind(blocks[j], "kv", j) if j else blocks[j]
+            source = (kv_idx - j + kv_count) % kv_count
+            pages = lax.dynamic_update_slice(
+                pages,
+                incoming.reshape(capacity, tokens, 2, -1),
+                (source * capacity, c * tokens, 0, 0),
+            )
+        return pages
+
     for c in range(CHUNKS):
         block = patch_pages[:, c * tokens : (c + 1) * tokens, :].reshape(pages_dev * tokens, -1)
         gathered = gather_features(block).astype(jnp.float32)
@@ -129,6 +183,9 @@
             )
             for j in range(1, tp_count)
         ]
+        if outgoing_all:
+            hidden, *outgoing_all = lax.optimization_barrier((hidden, *outgoing_all))
+            new_pages = exchange(new_pages, outgoing_all, c - 1)
         image_kv = jnp.dot(hidden, w_parts[0], preferred_element_type=jnp.float32)
         for part in arrived:
             image_kv = image_kv + part.astype(jnp.float32)
@@ -136,6 +193,7 @@
             image_kv.astype(jnp.bfloat16).reshape(pages_dev, tokens, -1), "section", 1
         )
         handed_parts.append(handed)
+        outgoing_all = []
         for j in range(kv_count):
             owner = (kv_idx + j) % kv_count
             placing = (
@@ -144,17 +202,17 @@
             outgoing = jnp.einsum(
                 "jp,ptf->jtf", placing, handed, preferred_element_type=jnp.float32
             ).astype(jnp.bfloat16)
-            incoming = from_behind(outgoing, "kv", j) if j else outgoing
-            source = (kv_idx - j) % kv_count
-            new_pages = lax.dynamic_update_slice(
-                new_pages,
-                incoming.reshape(capacity, tokens, 2, -1),
-                (source * capacity, c * tokens, 0, 0),
-            )
+            outgoing_all.append(outgoing)
+    cache, queries, *outgoing_all = lax.optimization_barrier((cache, queries, *outgoing_all))
+    new_pages = exchange(new_pages, outgoing_all, CHUNKS - 1)
     req_count = queries.shape[0]
     kv_heads_dev = cache.shape[3] // HEAD_DIM
     group_size = queries.shape[1] // HEAD_DIM // kv_heads_dev
-    query_grid = queries.reshape(req_count, kv_heads_dev, group_size, HEAD_DIM)
+    query_grid = (
+        queries.reshape(req_count, kv_heads_dev, group_size, HEAD_DIM)
+        .transpose(1, 0, 2, 3)
+        .reshape(kv_heads_dev, req_count * group_size, HEAD_DIM)
+    )
     lengths = cache_lengths[0]
     page_counts = (lengths + page_len - 1) // page_len
     starts = jnp.cumsum(page_counts) - page_counts
@@ -163,20 +221,30 @@
     inside = (within >= 0) & (within < page_counts[None, :])
     valid = jnp.where(inside, jnp.clip(lengths[None, :] - within * page_len, 0, page_len), 0)
     cache_mask = jnp.arange(page_len)[None, :, None] < valid[:, None, :]
-    cache_totals, cache_weighted = attend_part(query_grid, cache, cache_mask)
     image_of = (kv_idx * pages_dev + jnp.arange(pages_dev)) // IMAGE_PAGES
     image_hit = image_of[:, None] == jnp.arange(image_request.shape[1])[None, :]
     page_request = jnp.sum(jnp.where(image_hit, image_request[0][None, :], 0), axis=1)
     request_hit = page_request[:, None] == jnp.arange(req_count)[None, :]
     handed_mask = jnp.broadcast_to(request_hit[:, None, :], (pages_dev, tokens, req_count))
-    totals, weighted = cache_totals, cache_weighted
-    for handed in handed_parts:
-        part_totals, part_weighted = attend_part(
-            query_grid, handed.reshape(pages_dev, tokens, 2, -1), handed_mask
-        )
-        totals, weighted = totals + part_totals, weighted + part_weighted
-    totals, weighted = lax.psum((totals, weighted), "kv")
-    attended = (weighted / totals[..., None]).astype(jnp.bfloat16).reshape(req_count, -1)
+
+    def grouped(mask):
+        rows = mask.reshape(-1, req_count).T.astype(jnp.float32)
+        return jnp.repeat(rows, group_size, axis=0)
+
+    totals, weighted = attend_all(
+        query_grid,
+        [grouped(cache_mask)] + [grouped(handed_mask)] * CHUNKS,
+        [cache.reshape(-1, 2 * cache.shape[3])]
+        + [handed.reshape(pages_dev * tokens, -1) for handed in handed_parts],
+    )
+    totals, weighted = sum_over_kv(jnp.stack([totals, weighted]))
+    attended = (
+        (weighted / totals)
+        .astype(jnp.bfloat16)
+        .reshape(kv_heads_dev, req_count, group_size, HEAD_DIM)
+        .transpose(1, 0, 2, 3)
+        .reshape(req_count, -1)
+    )
     return (new_pages, attended)
 
 

time: 482 us -> 389 us (0.81); the launches traced: 473 us -> 385 us
  local copies, waits for them, and re-layouts: 154 us -> 73.2 us
  waiting for transfers between devices: 114 us -> 183 us
  blocking collectives: 59.1 us -> 0 us
  matrix products: 67.7 us -> 50 us
  starting transfers between devices: 55.5 us -> 48.7 us
    ppermute x28 -> x31, waiting for transfers between devices: 114 us -> 182 us  [from_behind(): return lax.ppermute(value, axis, pairs)]
    psum x1 -> x0, blocking collectives: 59.1 us -> none  [per_device(): totals, weighted = lax.psum((totals, weighted), 'kv')]
    slice x5 -> x0, local copies, waits for them, and re-layouts: 39.7 us -> none  [attend_part(): page_store[:, :, 0, :].reshape(slot_count * page_len, head_count, HEAD_DIM)]
    another operation x10 -> x0, local copies, waits for them, and re-layouts: 22 us -> none  [the longest x5 11.9 us: attend_part(): page_store[:, :, 0, :].reshape(slot_count * page_len, head_count, HEAD_DIM)]
    dot_general x16, matrix products: 18.4 us -> 7.89 us  [per_device(): jnp.einsum('jp,ptf->jtf', placing, handed, preferred_element_type=jnp.flo...]
    dot_general x10 -> x0, matrix products: 9.13 us -> none  [the longest x5 7.92 us: attend_part(): jnp.einsum('rkgd,tkd->rkgt', query_grid, keys, preferred_element_type=jnp...]
    unnamed x81 -> x72, local copies, waits for them, and re-layouts: 23.6 us -> 15.7 us
    ppermute x28 -> x31, starting transfers between devices: 55.5 us -> 48.7 us  [from_behind(): return lax.ppermute(value, axis, pairs)]
  transfers between devices with their start and end apart: 29 -> 32, of which waited for: 7 -> 14; matrix products, arithmetic and copies ran while one was open for 38% -> 28% of each run, Pallas kernels for 0% -> 0%
where the time goes in v2:
time: 389 us; the launch traced here: 385 us
  waiting for transfers between devices  183 us (47%)
  local copies, waits for them, and re-layouts  73.2 us (19%)
  matrix products  50 us (13%)
  starting transfers between devices  48.7 us (13%)
  between operations  15.1 us (4%)
  other arithmetic  11.7 us (3%)
    ppermute x31, waiting for transfers between devices, from_behind(): return lax.ppermute(value, axis, pairs)  182 us
    ppermute x31, starting transfers between devices, from_behind(): return lax.ppermute(value, axis, pairs)  48.7 us
    dynamic_update_slice x16, local copies, waits for them, and re-layouts, exchange(): lax.dynamic_update_slice(pages, incoming.reshape(capacity, tokens, 2, -1)...  19.2 us
    dot_general x4, matrix products, per_device(): jnp.dot(x_norm, full_w, preferred_element_type=jnp.float32) + b_proj  18.2 us
    unnamed x72, local copies, waits for them, and re-layouts  15.7 us
    dot_general x4, matrix products, per_device(): image_kv = jnp.dot(hidden, w_parts[0], preferred_element_type=jnp.float32)  13.1 us
    dot_general x4, matrix products, per_device(): jnp.dot(hidden, w_parts[j], preferred_element_type=jnp.float32)  10.7 us
    dynamic_slice x1, local copies, waits for them, and re-layouts, columns_of(): part = lax.dynamic_slice_in_dim(w_kv, member * width, width, axis=2)  9.45 us
  transfers between devices with their start and end apart: 32, of which 14 were waited for; matrix products, arithmetic and copies ran while one was open for 28% of the time, Pallas kernels for 0%

profile of v2, /device:TPU:25, one launch (start us, length us, event | category | flops | bytes accessed | tf_op | source)
XLA Modules:
  0.0 385.3 jit_solution(1268680139667000739)
XLA Ops:
  22.4 9.4 %constant_dynamic-slice_fusion.1 = (bf16[2304,2,512]{2,1,0:T(2,128)(2,1)}, bf16[2304,2,512]{2,1,0:T(2,128)(2,1)}) fusion(bf16[2304,2,1024]{2,1,0:T(2,128)(2,1)} %param.19, s32[]{:T(128)S(6)} %select_n.222, s32[]{:T(128)S(6)} %select_n.224), kind=kLoop, calls=%fused_computation.124 | loop fusion | bytes 18874376 | tf_op jit(solution)/shard_map/dynamic_slice | solution.py:44
  32.0 6.3 %copy.157 = bf16[288,8,2,512]{3,1,2,0:T(8,128)(2,1)} copy(bf16[288,8,2,512]{3,2,1,0:T(2,128)(2,1)} %bitcast.158) | data formatting | bytes 9437184
  38.3 3.7 copy.156
  45.1 9.2 %collective-permute-done.9 = bf16[512,576]{0,1:T(8,128)(2,1)S(1)} collective-permute-done((bf16[512,576]{0,1:T(8,128)(2,1)}, bf16[512,576]{0,1:T(8,128)(2,1)S(1)}, u32[]{:S(2)}, u32[]{:S(2)}) %collective-permute-start.9) | collective-permute-done | bytes 589856 | tf_op jit(solution)/shard_map/ppermute | solution.py:23
  55.3 11.7 %collective-permute-done.16 = bf16[512,576]{0,1:T(8,128)(2,1)} collective-permute-done((bf16[512,576]{0,1:T(8,128)(2,1)}, bf16[512,576]{0,1:T(8,128)(2,1)}, u32[]{:S(2)}, u32[]{:S(2)}) %collective-permute-start.16) | collective-permute-done | bytes 589856 | tf_op jit(solution)/shard_map/ppermute | solution.py:23
  77.2 7.2 %multiply_reduce_fusion.2 = (f32[512]{0:T(512)S(1)}, f32[512,2304]{1,0:T(8,128)S(1)}) fusion(f32[2304]{0:T(1024)S(1)} %copy-done.23, bf16[1152,2304]{1,0:T(8,128)(2,1)} %all-gather.2.cloned.1.call-done, f32[512]{0:T(512)S(1)} %add_rsqrt_fusion.5, f32[512]{0:T(512)S(1)} %broadcast_multiply_fusion.2, f32[1152]{0:T(1024)S(1)} %copy-done.24, ...), kind=kOutput, calls=%fused_computation.9 | convolution fusion | flops 2726755840 | bytes 11231232 | tf_op jit(solution)/shard_map/dot_general | solution.py:171
  85.6 3.7 multiply_reduce_fusion.3
  89.6 3.7 multiply_reduce_fusion.1
  94.6 3.7 multiply_reduce_fusion
  105.3 18.4 %collective-permute-done.4 = bf16[512,1024]{1,0:T(8,128)(2,1)S(1)} collective-permute-done((bf16[512,1024]{1,0:T(8,128)(2,1)S(1)}, bf16[512,1024]{1,0:T(8,128)(2,1)S(1)}, u32[]{:S(2)}, u32[]{:S(2)}) %collective-permute-start.4) | collective-permute-done | bytes 1048608 | tf_op jit(solution)/shard_map/ppermute | solution.py:23
  123.7 5.2 %add_convert_fusion.3 = bf16[512,1024]{1,0:T(8,128)(2,1)S(1)} fusion(bf16[512,1024]{1,0:T(8,128)(2,1)S(1)} %collective-permute-done.4, bf16[2304,1024]{1,0:T(8,128)(2,1)S(1)} %bitcast.166, f32[512,2304]{1,0:T(8,128)} %copy-done.27, f32[512]{0:T(512)S(1)} %add_rsqrt_fusion.4, f32[2304]{0:T(1024)S(1)} %copy-done.18), kind=kOutput, calls=%fused_computation.47 | convolution fusion | flops 2421030912 | bytes 11545600 | tf_op jit(solution)/shard_map/dot_general | solution.py:189
  129.5 4.8 %collective-permute-start.5 = (bf16[16,32,1024]{2,0,1:T(8,128)(2,1)S(1)}, bf16[16,32,1024]{2,0,1:T(8,128)(2,1)S(1)}, u32[]{:S(2)}, u32[]{:S(2)}) collective-permute-start(bf16[16,32,1024]{2,0,1:T(8,128)(2,1)S(1)} %copy.121), channel_id=1, source_target_pairs={{0,8},{8,16},{16,24},{24,0},{1,9},{9,17},{17,25},{25,1},{2,10},{10... | collective-permute-start | bytes 3145736 | tf_op jit(solution)/shard_map/ppermute | solution.py:23
  141.1 4.9 %collective-permute-done.5 = bf16[16,32,1024]{2,0,1:T(8,128)(2,1)S(1)} collective-permute-done((bf16[16,32,1024]{2,0,1:T(8,128)(2,1)S(1)}, bf16[16,32,1024]{2,0,1:T(8,128)(2,1)S(1)}, u32[]{:S(2)}, u32[]{:S(2)}) %collective-permute-start.5) | collective-permute-done | bytes 1048608 | tf_op jit(solution)/shard_map/ppermute | solution.py:23
  149.9 12.3 %collective-permute-done.11 = bf16[512,1024]{1,0:T(8,128)(2,1)S(1)} collective-permute-done((bf16[512,1024]{1,0:T(8,128)(2,1)S(1)}, bf16[512,1024]{1,0:T(8,128)(2,1)S(1)}, u32[]{:S(2)}, u32[]{:S(2)}) %collective-permute-start.11) | collective-permute-done | bytes 1048608 | tf_op jit(solution)/shard_map/ppermute | solution.py:23
  170.0 5.4 %broadcast_in_dim.19 = bf16[32,128,2,512]{3,2,1,0:T(2,128)(2,1)} broadcast(bf16[]{:T(256)} %constant.200.clone.1), dimensions={} | broadcast | bytes 8388610 | tf_op jit(solution)/shard_map/broadcast_in_dim | solution.py:147
  185.6 22.4 %collective-permute-start.19 = (bf16[16,32,1024]{2,0,1:T(8,128)(2,1)S(1)}, bf16[16,32,1024]{2,0,1:T(8,128)(2,1)S(1)}, u32[]{:S(2)}, u32[]{:S(2)}) collective-permute-start(bf16[16,32,1024]{2,0,1:T(8,128)(2,1)S(1)} %copy.139), channel_id=1, source_target_pairs={{0,8},{8,16},{16,24},{24,0},{1,9},{9,17},{17,25},{25,1},{2,10},{10... | collective-permute-start | bytes 3145736 | tf_op jit(solution)/shard_map/ppermute | solution.py:23
  208.0 3.6 collective-permute-done.7
  215.7 7.2 %collective-permute-done.13 = bf16[8,32,1024]{2,0,1:T(8,128)(2,1)S(1)} collective-permute-done((bf16[8,32,1024]{2,0,1:T(8,128)(2,1)S(1)}, bf16[8,32,1024]{2,0,1:T(8,128)(2,1)S(1)}, u32[]{:S(2)}, u32[]{:S(2)}) %collective-permute-start.13) | collective-permute-done | bytes 524320 | tf_op jit(solution)/shard_map/ppermute | solution.py:23
  224.1 32.4 %collective-permute-done.14 = bf16[8,32,1024]{2,0,1:T(8,128)(2,1)S(1)} collective-permute-done((bf16[8,32,1024]{2,0,1:T(8,128)(2,1)S(1)}, bf16[8,32,1024]{2,0,1:T(8,128)(2,1)S(1)}, u32[]{:S(2)}, u32[]{:S(2)}) %collective-permute-start.14) | collective-permute-done | bytes 524320 | tf_op jit(solution)/shard_map/ppermute | solution.py:23
  267.8 7.9 %collective-permute-done.20 = bf16[8,32,1024]{2,0,1:T(8,128)(2,1)S(1)} collective-permute-done((bf16[8,32,1024]{2,0,1:T(8,128)(2,1)S(1)}, bf16[8,32,1024]{2,0,1:T(8,128)(2,1)S(1)}, u32[]{:S(2)}, u32[]{:S(2)}) %collective-permute-start.20) | collective-permute-done | bytes 524320 | tf_op jit(solution)/shard_map/ppermute | solution.py:23
  277.0 29.4 %collective-permute-done.21 = bf16[8,32,1024]{2,0,1:T(8,128)(2,1)S(1)} collective-permute-done((bf16[8,32,1024]{2,0,1:T(8,128)(2,1)S(1)}, bf16[8,32,1024]{2,0,1:T(8,128)(2,1)S(1)}, u32[]{:S(2)}, u32[]{:S(2)}) %collective-permute-start.21) | collective-permute-done | bytes 524320 | tf_op jit(solution)/shard_map/ppermute | solution.py:23
  320.4 3.8 shard_map.140
  332.3 9.5 %collective-permute-done.25 = bf16[8,32,1024]{2,0,1:T(8,128)(2,1)S(1)} collective-permute-done((bf16[8,32,1024]{2,0,1:T(8,128)(2,1)}, bf16[8,32,1024]{2,0,1:T(8,128)(2,1)S(1)}, u32[]{:S(2)}, u32[]{:S(2)}) %collective-permute-start.25) | collective-permute-done | bytes 524320 | tf_op jit(solution)/shard_map/ppermute | solution.py:23
  343.0 32.9 %collective-permute-done.26 = bf16[8,32,1024]{2,0,1:T(8,128)(2,1)S(1)} collective-permute-done((bf16[8,32,1024]{2,0,1:T(8,128)(2,1)}, bf16[8,32,1024]{2,0,1:T(8,128)(2,1)S(1)}, u32[]{:S(2)}, u32[]{:S(2)}) %collective-permute-start.26) | collective-permute-done | bytes 524320 | tf_op jit(solution)/shard_map/ppermute | solution.py:23
  (240 shorter events, 111.7 us)
Async XLA Ops:
  7.2 69.9 %all-gather.2.cloned.1.call-start = ((), (), s32[]{:S(2)}) async-start(), calls=%async_computation | async-start | bytes 6635520 | tf_op jit(solution)/shard_map/all_gather | solution.py:137
  14.6 28.0 %collective-permute-start.2 = (bf16[512,576]{0,1:T(8,128)(2,1)}, bf16[512,576]{0,1:T(8,128)(2,1)S(1)}, u32[]{:S(2)}, u32[]{:S(2)}) collective-permute-start(bf16[512,576]{0,1:T(8,128)(2,1)} %copy.118), channel_id=1, source_target_pairs={{0,1},{1,0},{2,3},{3,2},{4,5},{5,4},{6,7},{7,6},{8,9},{9,8},{10,11... | collective-permute-start | bytes 1769480 | tf_op jit(solution)/shard_map/ppermute | solution.py:23
  17.9 25.8 %collective-permute-start = (bf16[512,576]{0,1:T(8,128)(2,1)}, bf16[512,576]{0,1:T(8,128)(2,1)}, u32[]{:S(2)}, u32[]{:S(2)}) collective-permute-start(bf16[512,576]{0,1:T(8,128)(2,1)} %copy.114), channel_id=1, source_target_pairs={{0,1},{1,0},{2,3},{3,2},{4,5},{5,4},{6,7},{7,6},{8,9},{9,8},{10,11... | collective-permute-start | bytes 1769480 | tf_op jit(solution)/shard_map/ppermute | solution.py:23
  19.3 35.0 %collective-permute-start.9 = (bf16[512,576]{0,1:T(8,128)(2,1)}, bf16[512,576]{0,1:T(8,128)(2,1)S(1)}, u32[]{:S(2)}, u32[]{:S(2)}) collective-permute-start(bf16[512,576]{0,1:T(8,128)(2,1)} %copy.127), channel_id=1, source_target_pairs={{0,1},{1,0},{2,3},{3,2},{4,5},{5,4},{6,7},{7,6},{8,9},{9,8},{10,11... | collective-permute-start | bytes 1769480 | tf_op jit(solution)/shard_map/ppermute | solution.py:23
  21.5 45.5 %collective-permute-start.16 = (bf16[512,576]{0,1:T(8,128)(2,1)}, bf16[512,576]{0,1:T(8,128)(2,1)}, u32[]{:S(2)}, u32[]{:S(2)}) collective-permute-start(bf16[512,576]{0,1:T(8,128)(2,1)} %copy.136), channel_id=1, source_target_pairs={{0,1},{1,0},{2,3},{3,2},{4,5},{5,4},{6,7},{7,6},{8,9},{9,8},{10,11... | collective-permute-start | bytes 1769480 | tf_op jit(solution)/shard_map/ppermute | solution.py:23
  84.3 14.3 %collective-permute-start.3 = (f32[512]{0:T(512)S(1)}, f32[512]{0:T(512)S(1)}, u32[]{:S(2)}, u32[]{:S(2)}) collective-permute-start(f32[512]{0:T(512)S(1)} %get-tuple-element.78), channel_id=1, source_target_pairs={{0,1},{1,0},{2,3},{3,2},{4,5},{5,4},{6,7},{7,6},{8,9},{9,8},{10,11... | collective-permute-start | bytes 6152 | tf_op jit(solution)/shard_map/ppermute | solution.py:23
  101.6 22.1 %collective-permute-start.4 = (bf16[512,1024]{1,0:T(8,128)(2,1)S(1)}, bf16[512,1024]{1,0:T(8,128)(2,1)S(1)}, u32[]{:S(2)}, u32[]{:S(2)}) collective-permute-start(bf16[512,1024]{1,0:T(8,128)(2,1)S(1)} %convolution_convert_fusion.3), channel_id=1, source_target_pairs={{0,1},{1,0},{2,3},{3,2},{4,5},{5,4},{6,7},{7,6},{8,9},{9,8},{10,11... | collective-permute-start | bytes 3145736 | tf_op jit(solution)/shard_map/ppermute | solution.py:23
  129.5 16.5 %collective-permute-start.5 = (bf16[16,32,1024]{2,0,1:T(8,128)(2,1)S(1)}, bf16[16,32,1024]{2,0,1:T(8,128)(2,1)S(1)}, u32[]{:S(2)}, u32[]{:S(2)}) collective-permute-start(bf16[16,32,1024]{2,0,1:T(8,128)(2,1)S(1)} %copy.121), channel_id=1, source_target_pairs={{0,8},{8,16},{16,24},{24,0},{1,9},{9,17},{17,25},{25,1},{2,10},{10... | collective-permute-start | bytes 3145736 | tf_op jit(solution)/shard_map/ppermute | solution.py:23
  136.9 25.2 %collective-permute-start.11 = (bf16[512,1024]{1,0:T(8,128)(2,1)S(1)}, bf16[512,1024]{1,0:T(8,128)(2,1)S(1)}, u32[]{:S(2)}, u32[]{:S(2)}) collective-permute-start(bf16[512,1024]{1,0:T(8,128)(2,1)S(1)} %convolution_convert_fusion.2), channel_id=1, source_target_pairs={{0,1},{1,0},{2,3},{3,2},{4,5},{5,4},{6,7},{7,6},{8,9},{9,8},{10,11... | collective-permute-start | bytes 3145736 | tf_op jit(solution)/shard_map/ppermute | solution.py:23
  140.9 43.7 %collective-permute-start.18 = (bf16[512,1024]{1,0:T(8,128)(2,1)S(1)}, bf16[512,1024]{1,0:T(8,128)(2,1)S(1)}, u32[]{:S(2)}, u32[]{:S(2)}) collective-permute-start(bf16[512,1024]{1,0:T(8,128)(2,1)S(1)} %convolution_convert_fusion.1), channel_id=1, source_target_pairs={{0,1},{1,0},{2,3},{3,2},{4,5},{5,4},{6,7},{7,6},{8,9},{9,8},{10,11... | collective-permute-start | bytes 3145736 | tf_op jit(solution)/shard_map/ppermute | solution.py:23
  163.1 16.3 %collective-permute-start.12 = (bf16[16,32,1024]{2,0,1:T(8,128)(2,1)S(1)}, bf16[16,32,1024]{2,0,1:T(8,128)(2,1)S(1)}, u32[]{:S(2)}, u32[]{:S(2)}) collective-permute-start(bf16[16,32,1024]{2,0,1:T(8,128)(2,1)S(1)} %copy.130), channel_id=1, source_target_pairs={{0,8},{8,16},{16,24},{24,0},{1,9},{9,17},{17,25},{25,1},{2,10},{10... | collective-permute-start | bytes 3145736 | tf_op jit(solution)/shard_map/ppermute | solution.py:23
  166.8 94.7 %collective-permute-start.23 = (bf16[512,1024]{1,0:T(8,128)(2,1)S(1)}, bf16[512,1024]{1,0:T(8,128)(2,1)S(1)}, u32[]{:S(2)}, u32[]{:S(2)}) collective-permute-start(bf16[512,1024]{1,0:T(8,128)(2,1)S(1)} %convolution_convert_fusion), channel_id=1, source_target_pairs={{0,1},{1,0},{2,3},{3,2},{4,5},{5,4},{6,7},{7,6},{8,9},{9,8},{10,11... | collective-permute-start | bytes 3145736 | tf_op jit(solution)/shard_map/ppermute | solution.py:23
  168.1 43.5 %collective-permute-start.7 = (bf16[8,32,1024]{2,0,1:T(8,128)(2,1)S(1)}, bf16[8,32,1024]{2,0,1:T(8,128)(2,1)S(1)}, u32[]{:S(2)}, u32[]{:S(2)}) collective-permute-start(bf16[8,32,1024]{2,0,1:T(8,128)(2,1)S(1)} %convolution_convert_fusion.17), channel_id=1, source_target_pairs={{0,4},{2,6},{4,0},{6,2},{1,5},{3,7},{5,1},{7,3},{8,12},{10,14},{12... | collective-permute-start | bytes 1572872 | tf_op jit(solution)/shard_map/ppermute | solution.py:23
  178.0 34.8 %collective-permute-start.8 = (bf16[8,32,1024]{2,0,1:T(8,128)(2,1)S(1)}, bf16[8,32,1024]{2,0,1:T(8,128)(2,1)S(1)}, u32[]{:S(2)}, u32[]{:S(2)}) collective-permute-start(bf16[8,32,1024]{2,0,1:T(8,128)(2,1)S(1)} %convolution_convert_fusion.16), channel_id=1, source_target_pairs={{0,6},{2,0},{4,2},{6,4},{1,7},{3,1},{5,3},{7,5},{8,14},{10,8},{12,... | collective-permute-start | bytes 1572872 | tf_op jit(solution)/shard_map/ppermute | solution.py:23
  185.6 72.1 %collective-permute-start.19 = (bf16[16,32,1024]{2,0,1:T(8,128)(2,1)S(1)}, bf16[16,32,1024]{2,0,1:T(8,128)(2,1)S(1)}, u32[]{:S(2)}, u32[]{:S(2)}) collective-permute-start(bf16[16,32,1024]{2,0,1:T(8,128)(2,1)S(1)} %copy.139), channel_id=1, source_target_pairs={{0,8},{8,16},{16,24},{24,0},{1,9},{9,17},{17,25},{25,1},{2,10},{10... | collective-permute-start | bytes 3145736 | tf_op jit(solution)/shard_map/ppermute | solution.py:23
  208.0 15.0 %collective-permute-start.13 = (bf16[8,32,1024]{2,0,1:T(8,128)(2,1)S(1)}, bf16[8,32,1024]{2,0,1:T(8,128)(2,1)S(1)}, u32[]{:S(2)}, u32[]{:S(2)}) collective-permute-start(bf16[8,32,1024]{2,0,1:T(8,128)(2,1)S(1)} %convolution_convert_fusion.14), channel_id=1, source_target_pairs={{0,2},{2,4},{4,6},{6,0},{1,3},{3,5},{5,7},{7,1},{8,10},{10,12},{12... | collective-permute-start | bytes 1572872 | tf_op jit(solution)/shard_map/ppermute | solution.py:23
  212.8 43.7 %collective-permute-start.14 = (bf16[8,32,1024]{2,0,1:T(8,128)(2,1)S(1)}, bf16[8,32,1024]{2,0,1:T(8,128)(2,1)S(1)}, u32[]{:S(2)}, u32[]{:S(2)}) collective-permute-start(bf16[8,32,1024]{2,0,1:T(8,128)(2,1)S(1)} %convolution_convert_fusion.13), channel_id=1, source_target_pairs={{0,4},{2,6},{4,0},{6,2},{1,5},{3,7},{5,1},{7,3},{8,12},{10,14},{12... | collective-permute-start | bytes 1572872 | tf_op jit(solution)/shard_map/ppermute | solution.py:23
  214.0 48.8 %collective-permute-start.15 = (bf16[8,32,1024]{2,0,1:T(8,128)(2,1)S(1)}, bf16[8,32,1024]{2,0,1:T(8,128)(2,1)S(1)}, u32[]{:S(2)}, u32[]{:S(2)}) collective-permute-start(bf16[8,32,1024]{2,0,1:T(8,128)(2,1)S(1)} %convolution_convert_fusion.12), channel_id=1, source_target_pairs={{0,6},{2,0},{4,2},{6,4},{1,7},{3,1},{5,3},{7,5},{8,14},{10,8},{12,... | collective-permute-start | bytes 1572872 | tf_op jit(solution)/shard_map/ppermute | solution.py:23
  261.5 14.3 %collective-permute-start.20 = (bf16[8,32,1024]{2,0,1:T(8,128)(2,1)S(1)}, bf16[8,32,1024]{2,0,1:T(8,128)(2,1)S(1)}, u32[]{:S(2)}, u32[]{:S(2)}) collective-permute-start(bf16[8,32,1024]{2,0,1:T(8,128)(2,1)S(1)} %convolution_convert_fusion.10), channel_id=1, source_target_pairs={{0,2},{2,4},{4,6},{6,0},{1,3},{3,5},{5,7},{7,1},{8,10},{10,12},{12... | collective-permute-start | bytes 1572872 | tf_op jit(solution)/shard_map/ppermute | solution.py:23
  262.5 46.2 %collective-permute-start.24 = (bf16[16,32,1024]{2,0,1:T(8,128)(2,1)S(1)}, bf16[16,32,1024]{2,0,1:T(8,128)(2,1)S(1)}, u32[]{:S(2)}, u32[]{:S(2)}) collective-permute-start(bf16[16,32,1024]{2,0,1:T(8,128)(2,1)S(1)} %copy.144), channel_id=1, source_target_pairs={{0,8},{8,16},{16,24},{24,0},{1,9},{9,17},{17,25},{25,1},{2,10},{10... | collective-permute-start | bytes 3145736 | tf_op jit(solution)/shard_map/ppermute | solution.py:23
  262.7 43.6 %collective-permute-start.21 = (bf16[8,32,1024]{2,0,1:T(8,128)(2,1)S(1)}, bf16[8,32,1024]{2,0,1:T(8,128)(2,1)S(1)}, u32[]{:S(2)}, u32[]{:S(2)}) collective-permute-start(bf16[8,32,1024]{2,0,1:T(8,128)(2,1)S(1)} %convolution_convert_fusion.9), channel_id=1, source_target_pairs={{0,4},{2,6},{4,0},{6,2},{1,5},{3,7},{5,1},{7,3},{8,12},{10,14},{12... | collective-permute-start | bytes 1572872 | tf_op jit(solution)/shard_map/ppermute | solution.py:23
  263.9 43.6 %collective-permute-start.22 = (bf16[8,32,1024]{2,0,1:T(8,128)(2,1)S(1)}, bf16[8,32,1024]{2,0,1:T(8,128)(2,1)S(1)}, u32[]{:S(2)}, u32[]{:S(2)}) collective-permute-start(bf16[8,32,1024]{2,0,1:T(8,128)(2,1)S(1)} %convolution_convert_fusion.8), channel_id=1, source_target_pairs={{0,6},{2,0},{4,2},{6,4},{1,7},{3,1},{5,3},{7,5},{8,14},{10,8},{12,... | collective-permute-start | bytes 1572872 | tf_op jit(solution)/shard_map/ppermute | solution.py:23
  330.1 45.8 %collective-permute-start.26 = (bf16[8,32,1024]{2,0,1:T(8,128)(2,1)}, bf16[8,32,1024]{2,0,1:T(8,128)(2,1)S(1)}, u32[]{:S(2)}, u32[]{:S(2)}) collective-permute-start(bf16[8,32,1024]{2,0,1:T(8,128)(2,1)} %convolution_convert_fusion.5), channel_id=1, source_target_pairs={{0,4},{2,6},{4,0},{6,2},{1,5},{3,7},{5,1},{7,3},{8,12},{10,14},{12... | collective-permute-start | bytes 1572872 | tf_op jit(solution)/shard_map/ppermute | solution.py:23
  331.3 45.8 %collective-permute-start.27 = (bf16[8,32,1024]{2,0,1:T(8,128)(2,1)}, bf16[8,32,1024]{2,0,1:T(8,128)(2,1)S(1)}, u32[]{:S(2)}, u32[]{:S(2)}) collective-permute-start(bf16[8,32,1024]{2,0,1:T(8,128)(2,1)} %convolution_convert_fusion.4), channel_id=1, source_target_pairs={{0,6},{2,0},{4,2},{6,4},{1,7},{3,1},{5,3},{7,5},{8,14},{10,8},{12,... | collective-permute-start | bytes 1572872 | tf_op jit(solution)/shard_map/ppermute | solution.py:23
  (42 other events, 393.8 us)
Sparse Core Ops, SparseCore 0:
  9.6 42.1 all-gather.1
